TPU v7x, 32 devices: a whole 2x2x4 slice. The times are simulated.
32 devices in a mesh: section: 2 (over core), head: 4 (over z), blk: 4 (over y, x).
Axes of the slice: x: 2, y: 2, z: 4, core: 2. Of those that a mesh axis runs over, the one named last changes fastest.
Arguments:
- section_input: bfloat16 [2, 8, 256, 1536], P('section', 'blk')
- modulation: bfloat16 [2, 8, 2, 1536], P('section', 'blk'), may hold values from -3 to 3
- attn_gate: bfloat16 [2, 8, 1536], P('section', 'blk'), may hold values from -12 to 12
- qkv_weight: bfloat16 [2, 1536, 3, 1536], P('section', None, None, 'head'), may hold values from -0.15625 to 0.15625
- out_weight: bfloat16 [2, 1536, 1536], P('section', 'head'), may hold values from -0.15625 to 0.15625
- kv_cache: bfloat16 [2, 8, 256, 4, 2, 1536], P('section', None, 'blk', None, None, 'head'), may hold values from -9 to 9
- text_kv: bfloat16 [2, 8, 154, 2, 1536], P('section', 'blk', None, None, 'head')
- text_len: int32 [8], P('blk'), may hold values from 4 to 154, as said below
- patch_order: int32 [4, 4], replicated, may hold values from 0 to 3, each once within a row
- final_mod: bfloat16 [8, 2, 1536], P('blk'), may hold values from -3 to 3
- final_weight: bfloat16 [1536, 64], replicated, may hold values from -0.15625 to 0.15625
- latent: float32 [4, 128, 128], P('blk', 'section'), may hold values from -6 to 6
Outputs:
- section_output: bfloat16 [2, 8, 256, 1536], P('section', 'blk', None, 'head')
- cache_patch: bfloat16 [2, 8, 256, 2, 1536], P('section', None, 'blk', None, 'head')
- latent_next: float32 [4, 128, 128], P('blk', 'section')
Inputs may be any that keep to these rules, and one draw needn't show every extreme that they name: `text_len`: sequence 0 uses all 154 text positions. `patch_order`: each row is a permutation of the 4 patches.
All inputs are finite; a program needn't handle non-finite values.
Results may differ from a plain program's by a relative error of at most 0.0092.
Values may be sent and summed in bfloat16 or wider, within the bound.
A program may use at most 128 MiB of HBM per device.

v0:
```python
import jax
import jax.numpy as jnp
from jax import lax
from jax.sharding import PartitionSpec as P

HEAD_DIM = 64
norm_eps = 1e-06
guidance = 4.0
euler_step = -0.25


def passed_along(shard, axis, by):
    devices = lax.axis_size(axis)
    return lax.ppermute(shard, axis, [(i, (i + by) % devices) for i in range(devices)])


def layer_norm(values):
    row_mean = jnp.mean(values, axis=-1, keepdims=True)
    centered = values - row_mean
    row_var = jnp.mean(centered * centered, axis=-1, keepdims=True)
    return centered / jnp.sqrt(row_var + norm_eps)


def piece_scores(query_heads, key_piece, counted_piece):
    seq_dev = key_piece.shape[0]
    head_count = query_heads.shape[2]
    key_heads = key_piece.reshape(seq_dev, -1, head_count, HEAD_DIM)
    scores = jnp.einsum(
        "sqhd,skhd->shqk", query_heads, key_heads, preferred_element_type=jnp.float32
    ) * HEAD_DIM ** (-0.5)
    if counted_piece is not None:
        scores = jnp.where(counted_piece[:, None, None, :], scores, -1e30)
    return scores


def piece_values(probs_piece, value_piece, head_count):
    seq_dev = value_piece.shape[0]
    value_heads = value_piece.reshape(seq_dev, -1, head_count, HEAD_DIM)
    return jnp.einsum(
        "shqk,skhd->sqhd", probs_piece, value_heads, preferred_element_type=jnp.float32
    )


def shards(
    section_input,
    modulation,
    attn_gate,
    qkv_weight,
    out_weight,
    kv_cache,
    text_kv,
    text_len,
    patch_order,
    final_mod,
    final_weight,
    latent,
):
    section_index = lax.axis_index("section")
    seq_patch = jnp.repeat(
        lax.dynamic_index_in_dim(patch_order, section_index, 1, keepdims=False), 2
    )
    hidden_in = section_input[0]
    seq_dev, patch_rows, model_width = hidden_in.shape
    own_patch = lax.dynamic_slice_in_dim(seq_patch, lax.axis_index("blk") * seq_dev, seq_dev, 0)
    hidden_wide = hidden_in.astype(jnp.float32)
    shift_scale = modulation[0].astype(jnp.float32)
    normed = (layer_norm(hidden_wide) * (1.0 + shift_scale[:, 1:2]) + shift_scale[:, 0:1]).astype(
        jnp.bfloat16
    )
    group_width = qkv_weight.shape[3]
    projected = jnp.dot(
        normed.reshape(seq_dev * patch_rows, model_width),
        qkv_weight[0].reshape(model_width, 3 * group_width),
        preferred_element_type=jnp.float32,
    ).astype(jnp.bfloat16)
    projected = projected.reshape(seq_dev, patch_rows, 3, group_width)
    queries = projected[:, :, 0]
    key_new = projected[:, :, 1]
    value_new = projected[:, :, 2]
    fresh_kv = jnp.stack([key_new, value_new], axis=2)
    refreshed = lax.all_to_all(fresh_kv, "blk", split_axis=1, concat_axis=0, tiled=True)
    local_cache = kv_cache[0]
    patch_count = local_cache.shape[2]
    fetched = lax.all_to_all(local_cache, "blk", split_axis=0, concat_axis=1, tiled=True)
    keep_patch = jnp.arange(patch_count, dtype=jnp.int32)[None, :] != own_patch[:, None]
    stale_counted = jnp.tile(keep_patch, (1, patch_rows))
    stale_keys = fetched[:, :, :, 0].reshape(seq_dev, -1, group_width)
    stale_values = fetched[:, :, :, 1].reshape(seq_dev, -1, group_width)
    text_local = text_kv[0]
    text_count = text_local.shape[1]
    text_counted = jnp.arange(text_count, dtype=jnp.int32)[None, :] < text_len[:, None]
    head_count = group_width // HEAD_DIM
    query_heads = queries.reshape(seq_dev, patch_rows, head_count, HEAD_DIM)
    text_scores = piece_scores(query_heads, text_local[:, :, 0], text_counted)
    fresh_scores = piece_scores(query_heads, key_new, None)
    stale_scores = piece_scores(query_heads, stale_keys, stale_counted)
    row_max = jnp.maximum(
        jnp.maximum(
            jnp.max(text_scores, axis=-1, keepdims=True),
            jnp.max(fresh_scores, axis=-1, keepdims=True),
        ),
        jnp.max(stale_scores, axis=-1, keepdims=True),
    )
    text_weights = jnp.exp(text_scores - row_max)
    fresh_weights = jnp.exp(fresh_scores - row_max)
    stale_weights = jnp.exp(stale_scores - row_max)
    total = (
        jnp.sum(text_weights, axis=-1, keepdims=True)
        + jnp.sum(fresh_weights, axis=-1, keepdims=True)
        + jnp.sum(stale_weights, axis=-1, keepdims=True)
    )
    text_probs = (text_weights / total).astype(jnp.bfloat16)
    fresh_probs = (fresh_weights / total).astype(jnp.bfloat16)
    stale_probs = (stale_weights / total).astype(jnp.bfloat16)
    attended_wide = (
        piece_values(text_probs, text_local[:, :, 1], head_count)
        + piece_values(fresh_probs, value_new, head_count)
        + piece_values(stale_probs, stale_values, head_count)
    )
    attended = attended_wide.astype(jnp.bfloat16)
    partial_value = jnp.dot(
        attended.reshape(seq_dev * patch_rows, group_width),
        out_weight[0],
        preferred_element_type=jnp.float32,
    )
    gate_wide = attn_gate[0].astype(jnp.float32)[:, None, :]
    share_width = model_width // lax.axis_size("head")
    share_start = lax.axis_index("head") * share_width
    half_rows = patch_rows // 2
    share_sum = lax.psum_scatter(
        partial_value.reshape(seq_dev, patch_rows, model_width).astype(jnp.bfloat16),
        "head",
        scatter_dimension=2,
        tiled=True,
    ).astype(jnp.float32)
    own_hidden = lax.dynamic_slice_in_dim(hidden_wide, share_start, share_width, 2)
    own_gate = lax.dynamic_slice_in_dim(gate_wide, share_start, share_width, 2)
    layer_out = (own_hidden + own_gate * share_sum).astype(jnp.bfloat16)
    received = passed_along(layer_out, "section", 1)
    last_layer = jnp.where(section_index == 0, received, layer_out)
    last_half = lax.dynamic_slice_in_dim(last_layer, section_index * half_rows, half_rows, 1)
    final_rows = lax.all_gather(last_half, "head", axis=2, tiled=True)
    final_shift = final_mod.astype(jnp.float32)
    final_normed = (
        layer_norm(final_rows.astype(jnp.float32)) * (1.0 + final_shift[:, 1:2])
        + final_shift[:, 0:1]
    ).astype(jnp.bfloat16)
    velocity = jnp.dot(
        final_normed.reshape(seq_dev * half_rows, model_width),
        final_weight,
        preferred_element_type=jnp.float32,
    )
    velocity = velocity.reshape(seq_dev // 2, 2, -1)
    guided = velocity[:, 1] + guidance * (velocity[:, 0] - velocity[:, 1])
    latent_next = latent + euler_step * guided.reshape(latent.shape)
    return (received[None], refreshed[None], latent_next)


def solution(mesh):
    placed = (
        P("section", "blk", None, None),
        P("section", "blk", None, None),
        P("section", "blk", None),
        P("section", None, None, "head"),
        P("section", "head", None),
        P("section", None, "blk", None, None, "head"),
        P("section", "blk", None, None, "head"),
        P("blk"),
        P(),
        P("blk", None, None),
        P(),
        P("blk", "section", None),
    )
    return jax.shard_map(
        shards,
        mesh=mesh,
        in_specs=placed,
        out_specs=(
            P("section", "blk", None, "head"),
            P("section", None, "blk", None, "head"),
            P("blk", "section", None),
        ),
        check_vma=False,
    )
```

profile of v0, /device:TPU:0, one launch (start us, length us, event | category | flops | bytes accessed | tf_op | source)
XLA Modules:
  0.0 174.6 jit_solution(1458555649823151610)
XLA Ops:
  7.2 5.4 %all-to-all-start = ((bf16[8,64,4,2,384]{4,3,2,1,0:T(2,128)(2,1)}), bf16[8,64,4,2,384]{4,3,2,1,0:T(2,128)(2,1)}, u32[]{:S(2)}, u32[]{:S(2)}) async-start(bf16[8,64,4,2,384]{4,3,2,1,0:T(2,128)(2,1)} %bitcast.90), calls=%async_computation | async-start | bytes 6291456 | tf_op jit(solution)/shard_map/all_to_all | solution.py:84
  13.8 0.5 multiply_reduce_fusion
  14.3 6.1 %copy.85 = bf16[1,1536,3,384]{1,3,2,0:T(8,128)(2,1)} copy(bf16[1,1536,3,384]{3,1,2,0:T(8,128)(2,1)} %param.15) | data formatting | bytes 7077888 | tf_op args[3]
  20.4 0.7 add_convert_fusion
  21.1 5.2 %convolution_convert_fusion = bf16[512,1152]{1,0:T(8,128)(2,1)} fusion(bf16[512,1536]{1,0:T(8,128)(2,1)S(1)} %bitcast.95, bf16[1536,1152]{0,1:T(8,128)(2,1)} %bitcast.89), kind=kOutput, calls=%fused_computation.14 | convolution fusion | flops 1812529152 | bytes 6291456 | tf_op jit(solution)/shard_map/dot_general | solution.py:71
  26.3 2.4 %copy.86 = bf16[512,1152]{0,1:T(8,128)(2,1)} copy(bf16[512,1152]{1,0:T(8,128)(2,1)} %convolution_convert_fusion) | data formatting | bytes 2359296 | tf_op jit(solution)/shard_map/convert_element_type | solution.py:75
  28.7 3.7 %reshape.237 = bf16[2,256,3,384]{1,0,3,2:T(2,128)(2,1)} reshape(bf16[512,1152]{0,1:T(8,128)(2,1)} %copy.86) | data formatting | bytes 2359296 | tf_op jit(solution)/shard_map/reshape | solution.py:76
  32.4 2.1 %fusion.35 = (bf16[2,256,1,384]{1,0,3,2:T(2,128)(2,1)S(1)}, bf16[2,256,1,384]{1,0,3,2:T(2,128)(2,1)S(1)}, bf16[2,256,1,384]{1,0,3,2:T(2,128)(2,1)S(1)}) fusion(bf16[2,256,3,384]{1,0,3,2:T(2,128)(2,1)} %reshape.237), kind=kLoop, calls=%fused_computation.71 | loop fusion | bytes 2359296 | tf_op jit(solution)/shard_map/slice | solution.py:79
  34.6 0.8 copy.89
  35.4 1.6 fusion.36
  37.0 2.0 %copy.88 = bf16[2,154,1,384]{1,3,0,2:T(8,128)(2,1)} copy(bf16[2,154,1,384]{3,2,1,0:T(2,128)(2,1)} %get-tuple-element.18) | data formatting | bytes 473088 | tf_op jit(solution)/shard_map/slice | solution.py:94
  38.9 0.8 copy.93
  39.7 2.0 %copy.92 = bf16[2,154,1,384]{1,3,0,2:T(8,128)(2,1)} copy(bf16[2,154,1,384]{3,2,1,0:T(2,128)(2,1)} %get-tuple-element.17) | data formatting | bytes 473088 | tf_op jit(solution)/shard_map/slice | solution.py:116
  41.9 3.5 %fusion.9 = (f32[2,6,256]{2,1,0:T(8,128)}, f32[2,6,256,154]{2,3,1,0:T(8,128)}) fusion(pred[2,154]{1,0:T(4,128)(4,1)S(1)} %iota_compare_fusion, bf16[2,256,6,64]{1,3,2,0:T(8,128)(2,1)S(1)} %bitcast.86, bf16[2,154,6,64]{1,3,2,0:T(8,128)(2,1)} %bitcast.96), kind=kOutput, calls=%fused_computation.26 | convolution fusion | flops 61971456 | bytes 2534708 | tf_op jit(solution)/shard_map/sqhd,skhd->shqk/dot_general | solution.py:28
  45.3 2.9 %multiply_reduce_fusion.1 = (f32[2,6,256]{2,1,0:T(8,128)}, f32[2,6,256,256]{2,3,1,0:T(8,128)}) fusion(bf16[2,256,6,64]{1,3,2,0:T(8,128)(2,1)S(1)} %bitcast.87, bf16[2,256,6,64]{1,3,2,0:T(8,128)(2,1)S(1)} %bitcast.98), kind=kOutput, calls=%fused_computation.16 | convolution fusion | flops 102233088 | bytes 3944448 | tf_op jit(solution)/shard_map/sqhd,skhd->shqk/dot_general | solution.py:28
  48.2 1.6 all-to-all-done
  49.8 3.4 %copy.90 = bf16[2,4,64,4,2,384]{5,3,2,1,0,4:T(4,128)(2,1)S(1)} copy(bf16[2,4,64,4,2,384]{5,4,3,2,0,1:T(2,128)(2,1)} %bitcast.13) | data formatting | bytes 6291456 | tf_op jit(solution)/shard_map/all_to_all | solution.py:84
  53.2 2.8 %fusion.34 = (bf16[2,256,4,1,384]{4,2,1,0,3:T(4,128)(2,1)}, bf16[2,256,4,1,384]{4,2,1,0,3:T(4,128)(2,1)}) fusion(bf16[2,256,4,2,384]{4,2,1,0,3:T(4,128)(2,1)S(1)} %bitcast.83), kind=kLoop, calls=%fused_computation.70 | loop fusion | bytes 6291456 | tf_op jit(solution)/shard_map/slice | solution.py:87
  56.0 6.0 %reshape_reshape_squeeze.6 = bf16[2,1024,6,64]{3,2,1,0:T(8,128)(2,1)} reshape(bf16[2,256,4,1,384]{4,2,1,0,3:T(4,128)(2,1)} %get-tuple-element.12) | data formatting | bytes 3145728 | tf_op jit(solution)/shard_map/reshape;reshape;squeeze | solution.py:27
  62.0 4.4 %fusion = (f32[2,6,256]{2,1,0:T(8,128)S(1)}, f32[2,6,256,1024]{3,2,1,0:T(8,128)S(1)}) fusion(pred[2,1024]{1,0:T(4,128)(4,1)S(1)} %tile.9, bf16[2,256,6,64]{1,3,2,0:T(8,128)(2,1)S(1)} %bitcast.88, bf16[2,1024,6,64]{3,2,1,0:T(8,128)(2,1)} %reshape_reshape_squeeze.6), kind=kOutput, calls=%fused_computation.3 | convolution fusion | flops 412087296 | bytes 14563328 | tf_op jit(solution)/shard_map/sqhd,skhd->shqk/dot_general | solution.py:28
  66.5 3.3 %fusion.1 = f32[2,6,256]{2,1,0:T(8,128)S(1)} fusion(f32[2,6,256,1024]{3,2,1,0:T(8,128)S(1)} %get-tuple-element.24, f32[2,6,256]{2,1,0:T(8,128)S(1)} %maximum_maximum_fusion, pred[2,1024]{1,0:T(4,128)(4,1)S(1)} %tile.9), kind=kLoop, calls=%fused_computation.4 | loop fusion | flops 12579840 | bytes 12609536 | tf_op jit(solution)/shard_map/reduce_sum | solution.py:110
  69.8 2.0 %copy-done.1 = f32[2,6,256,1024]{3,2,1,0:T(8,128)} copy-done((f32[2,6,256,1024]{3,2,1,0:T(8,128)}, f32[2,6,256,1024]{3,2,1,0:T(8,128)S(1)}, u32[]{:S(2)}) %copy-start.1) | copy-done | bytes 12582936
  71.8 0.5 fusion.6
  72.3 1.0 copy-done.5
  73.4 0.5 fusion.15
  73.9 6.1 %reshape_reshape_squeeze.7 = bf16[2,1024,6,64]{3,2,1,0:T(8,128)(2,1)} reshape(bf16[2,256,4,1,384]{4,2,1,0,3:T(4,128)(2,1)} %get-tuple-element.13) | data formatting | bytes 3145728 | tf_op jit(solution)/shard_map/reshape;reshape;squeeze | solution.py:38
  80.0 2.8 %fusion.16 = f32[2,256,6,64]{1,3,2,0:T(8,128)S(1)} fusion(bf16[2,256,6,64]{1,3,2,0:T(8,128)(2,1)S(1)} %bitcast.101, f32[2,6,256,256]{2,3,1,0:T(8,128)} %get-tuple-element.28, f32[2,6,256]{2,1,0:T(8,128)S(1)} %add_add_fusion, f32[2,6,256]{2,1,0:T(8,128)S(1)} %maximum_maximum_fusion), kind=kOutput, calls=%fused_computation.33 | convolution fusion | flops 103809024 | bytes 4349952 | tf_op jit(solution)/shard_map/shqk,skhd->sqhd/dot_general | solution.py:39
  82.8 2.7 %copy-done.2 = f32[2,6,256,1024]{3,2,1,0:T(8,128)S(1)} copy-done((f32[2,6,256,1024]{3,2,1,0:T(8,128)S(1)}, f32[2,6,256,1024]{3,2,1,0:T(8,128)}, u32[]{:S(2)}) %copy-start.2) | copy-done | bytes 12582936
  85.5 5.7 %fusion.19 = f32[2,256,6,64]{1,3,2,0:T(8,128)S(1)} fusion(bf16[2,1024,6,64]{3,2,1,0:T(8,128)(2,1)} %reshape_reshape_squeeze.7, f32[2,6,256,1024]{3,2,1,0:T(8,128)S(1)} %copy-done.2, f32[2,6,256]{2,1,0:T(8,128)S(1)} %add_add_fusion, f32[2,6,256]{2,1,0:T(8,128)S(1)} %maximum_maximum_fusion, pred[2,1024]{1,0:T(4,128)(4,1)S(1)} %tile.9), kind=kOutput, calls=%fused_computation.37 | convolution fusion | flops 418381824 | bytes 14968832 | tf_op jit(solution)/shard_map/shqk,skhd->sqhd/dot_general | solution.py:39
  91.2 0.7 fusion.22
  91.9 2.2 %convolution_convert_fusion.1 = bf16[2,256,1536]{2,1,0:T(8,128)(2,1)} fusion(bf16[2,256,384]{1,2,0:T(8,128)(2,1)S(1)} %bitcast.99, bf16[1,384,1536]{2,1,0:T(8,128)(2,1)S(1)} %copy-done), kind=kOutput, calls=%fused_computation.15 | convolution fusion | flops 604766208 | bytes 3145728 | tf_op jit(solution)/shard_map/dot_general | solution.py:121
  94.1 4.9 %copy.105 = bf16[2,256,1536]{1,0,2:T(2,128)(2,1)} copy(bf16[2,256,1536]{2,1,0:T(8,128)(2,1)} %convolution_convert_fusion.1) | data formatting | bytes 3145728
  99.0 3.0 %copy.111 = bf16[192,8,2,256]{3,1,2,0:T(8,128)(2,1)} copy(bf16[192,8,2,256]{3,2,1,0:T(2,128)(2,1)} %bitcast.85) | data formatting | bytes 3145728
  102.0 2.9 %copy.97 = bf16[2,256,2,384]{3,2,0,1:T(2,128)(2,1)} copy(bf16[2,256,2,384]{1,0,3,2:T(2,128)(2,1)S(1)} %slice-done) | data formatting | bytes 1572864 | tf_op jit(solution)/shard_map/stack | solution.py:80
  104.9 3.6 %all-to-all-start.1 = ((bf16[2,256,2,384]{3,2,0,1:T(2,128)(2,1)}), bf16[2,256,2,384]{3,2,0,1:T(2,128)(2,1)S(1)}, u32[]{:S(2)}, u32[]{:S(2)}) async-start(bf16[2,256,2,384]{3,2,0,1:T(2,128)(2,1)} %copy.97), calls=%async_computation.1 | async-start | bytes 1572864 | tf_op jit(solution)/shard_map/all_to_all | solution.py:81
  108.5 2.1 %convert_element_type.70 = f32[1,2,256,1536]{3,2,1,0:T(8,128)} convert(bf16[1,2,256,1536]{3,2,1,0:T(8,128)(2,1)S(1)} %copy-done.3) | non-fusion elementwise | flops 786432 | bytes 4718592 | tf_op jit(solution)/shard_map/convert_element_type | solution.py:65
  110.6 0.7 convert_bitcast_fusion
  111.3 27.1 %reduce-scatter.4.cloned.1.call-done = bf16[384,512]{1,0:T(8,128)(2,1)} async-done(((bf16[1536,512]{1,0:T(8,128)(2,1)}), bf16[384,512]{1,0:T(8,128)(2,1)}) %reduce-scatter.4.cloned.1.call-update) | async-done | bytes 393232
  138.4 1.1 reshape.244
  139.5 0.7 copy.106
  140.2 2.0 %fusion.28 = bf16[2,256,384]{2,1,0:T(8,128)(2,1)} fusion(bf16[2,256,384]{2,1,0:T(8,128)(2,1)S(1)} %copy.106, f32[1,2,256,1536]{3,2,1,0:T(8,128)} %convert_element_type.70, s32[]{:T(128)S(6)} %select_n.30, f32[2,384]{1,0:T(2,128)S(1)} %convert_bitcast_fusion), kind=kLoop, calls=%fused_computation.45 | loop fusion | flops 786432 | bytes 1575940 | tf_op jit(solution)/shard_map/convert_element_type | solution.py:138
  142.2 0.6 copy_bitcast_fusion
  143.0 1.7 copy.101
  144.7 1.1 dynamic-slice_select_fusion
  145.8 18.0 %all_gather.3 = bf16[2,128,1536]{2,1,0:T(8,128)(2,1)S(1)} all-gather(bf16[2,128,384]{2,1,0:T(8,128)(2,1)S(1)} %dynamic-slice_select_fusion), channel_id=1, replica_groups=mesh['section'=2,'head'=4,'blk'=4] {'head'}, dimensions={2}, use_global_device_ids=true | all-gather | bytes 983040 | tf_op jit(solution)/shard_map/all_gather | solution.py:142
  164.4 0.4 fusion.13
  165.3 0.6 multiply_add_fusion
  165.9 1.8 %copy.125 = bf16[1,2,256,384]{3,2,1,0:T(8,128)(2,1)} copy(bf16[1,2,256,384]{3,2,1,0:T(8,128)(2,1)} %bitcast.23) | data formatting | bytes 786432
  (73 shorter events, 2.6 us)
Async XLA Ops:
  7.2 84.8 %copy-start = (bf16[1,384,1536]{2,1,0:T(8,128)(2,1)S(1)}, bf16[1,384,1536]{2,1,0:T(8,128)(2,1)}, u32[]{:S(2)}) copy-start(bf16[1,384,1536]{2,1,0:T(8,128)(2,1)} %param.16) | copy-start | bytes 3538948
  7.2 5.5 %copy-start.18 = (s32[4,4]{1,0:T(4,128)S(1)}, s32[4,4]{1,0:T(4,128)}, u32[]{:S(2)}) copy-start(s32[4,4]{1,0:T(4,128)} %param.20) | copy-start | bytes 196
  7.2 6.2 %copy-start.17 = (bf16[1,2,2,1536]{3,2,1,0:T(2,128)(2,1)S(1)}, bf16[1,2,2,1536]{3,2,1,0:T(2,128)(2,1)}, u32[]{:S(2)}) copy-start(bf16[1,2,2,1536]{3,2,1,0:T(2,128)(2,1)} %param.13) | copy-start | bytes 36868
  7.2 6.3 %copy-start.3 = (bf16[1,2,256,1536]{3,2,1,0:T(8,128)(2,1)S(1)}, bf16[1,2,256,1536]{3,2,1,0:T(8,128)(2,1)}, u32[]{:S(2)}) copy-start(bf16[1,2,256,1536]{3,2,1,0:T(8,128)(2,1)} %param.12) | copy-start | bytes 4718596
  7.2 42.6 %all-to-all-start = ((bf16[8,64,4,2,384]{4,3,2,1,0:T(2,128)(2,1)}), bf16[8,64,4,2,384]{4,3,2,1,0:T(2,128)(2,1)}, u32[]{:S(2)}, u32[]{:S(2)}) async-start(bf16[8,64,4,2,384]{4,3,2,1,0:T(2,128)(2,1)} %bitcast.90), calls=%async_computation | async-start | bytes 6291456 | tf_op jit(solution)/shard_map/all_to_all | solution.py:84
  12.6 125.8 %reduce-scatter.4.cloned.1.call-start = ((), (), s32[]{:S(2)}) async-start(), calls=%async_computation.3 | async-start | bytes 1966080
  32.4 3.0 %copy-start.7 = (bf16[1,2,154,2,384]{4,3,2,1,0:T(2,128)(2,1)S(1)}, bf16[1,2,154,2,384]{4,3,2,1,0:T(2,128)(2,1)}, u32[]{:S(2)}) copy-start(bf16[1,2,154,2,384]{4,3,2,1,0:T(2,128)(2,1)} %param.18) | copy-start | bytes 1419268
  34.5 7.3 %copy-start.19 = (s32[2]{0:T(128)S(1)}, s32[2]{0:T(128)}, u32[]{:S(2)}) copy-start(s32[2]{0:T(128)} %param.19) | copy-start | bytes 28
  39.7 5.6 %copy-start.8 = (bf16[2,256,1,384]{1,3,0,2:T(8,128)(2,1)S(1)}, bf16[2,256,1,384]{1,3,0,2:T(8,128)(2,1)}, u32[]{:S(2)}) copy-start(bf16[2,256,1,384]{1,3,0,2:T(8,128)(2,1)} %copy.89) | copy-start | bytes 1179652
  62.0 4.5 %copy-start.12 = (f32[2,6,256]{2,1,0:T(8,128)S(1)}, f32[2,6,256]{2,1,0:T(8,128)}, u32[]{:S(2)}) copy-start(f32[2,6,256]{2,1,0:T(8,128)} %get-tuple-element.25) | copy-start | bytes 36868
  62.0 4.5 %copy-start.13 = (f32[2,6,256]{2,1,0:T(8,128)S(1)}, f32[2,6,256]{2,1,0:T(8,128)}, u32[]{:S(2)}) copy-start(f32[2,6,256]{2,1,0:T(8,128)} %get-tuple-element.27) | copy-start | bytes 36868
  66.5 5.3 %copy-start.1 = (f32[2,6,256,1024]{3,2,1,0:T(8,128)}, f32[2,6,256,1024]{3,2,1,0:T(8,128)S(1)}, u32[]{:S(2)}) copy-start(f32[2,6,256,1024]{3,2,1,0:T(8,128)S(1)} %get-tuple-element.24) | copy-start | bytes 37748740
  66.5 5.3 %copy-start.4 = (f32[2,6,256,256]{2,3,1,0:T(8,128)S(1)}, f32[2,6,256,256]{2,3,1,0:T(8,128)}, u32[]{:S(2)}) copy-start(f32[2,6,256,256]{2,3,1,0:T(8,128)} %get-tuple-element.28) | copy-start | bytes 9437188
  71.8 1.5 copy-start.5
  73.8 6.2 %copy-start.10 = (bf16[2,256,1,384]{1,3,0,2:T(8,128)(2,1)S(1)}, bf16[2,256,1,384]{1,3,0,2:T(8,128)(2,1)}, u32[]{:S(2)}) copy-start(bf16[2,256,1,384]{1,3,0,2:T(8,128)(2,1)} %copy.93) | copy-start | bytes 1179652
  80.0 5.5 %copy-start.2 = (f32[2,6,256,1024]{3,2,1,0:T(8,128)S(1)}, f32[2,6,256,1024]{3,2,1,0:T(8,128)}, u32[]{:S(2)}) copy-start(f32[2,6,256,1024]{3,2,1,0:T(8,128)} %copy-done.1) | copy-start | bytes 37748740
  85.5 5.7 %copy-start.6 = (f32[2,6,256,154]{2,3,1,0:T(8,128)S(1)}, f32[2,6,256,154]{2,3,1,0:T(8,128)}, u32[]{:S(2)}) copy-start(f32[2,6,256,154]{2,3,1,0:T(8,128)} %get-tuple-element.26) | copy-start | bytes 5677060
  85.5 5.7 %copy-start.9 = (bf16[2,154,1,384]{1,3,0,2:T(8,128)(2,1)S(1)}, bf16[2,154,1,384]{1,3,0,2:T(8,128)(2,1)}, u32[]{:S(2)}) copy-start(bf16[2,154,1,384]{1,3,0,2:T(8,128)(2,1)} %copy.92) | copy-start | bytes 709636
  99.0 3.0 %slice-start = ((bf16[2,256,3,384]{1,0,3,2:T(2,128)(2,1)}), bf16[2,256,2,384]{1,0,3,2:T(2,128)(2,1)S(1)}, s32[]{:S(2)}) async-start(bf16[2,256,3,384]{1,0,3,2:T(2,128)(2,1)} %reshape.237), calls=%async_computation.4 | async-start | bytes 1572864 | tf_op jit(solution)/shard_map/stack | solution.py:80
  104.9 5.7 %copy-start.15 = (bf16[2,2,1536]{2,1,0:T(2,128)(2,1)S(1)}, bf16[2,2,1536]{2,1,0:T(2,128)(2,1)}, u32[]{:S(2)}) copy-start(bf16[2,2,1536]{2,1,0:T(2,128)(2,1)} %param.21) | copy-start | bytes 36868
  104.9 37.9 %all-to-all-start.1 = ((bf16[2,256,2,384]{3,2,0,1:T(2,128)(2,1)}), bf16[2,256,2,384]{3,2,0,1:T(2,128)(2,1)S(1)}, u32[]{:S(2)}, u32[]{:S(2)}) async-start(bf16[2,256,2,384]{3,2,0,1:T(2,128)(2,1)} %copy.97), calls=%async_computation.1 | async-start | bytes 1572864 | tf_op jit(solution)/shard_map/all_to_all | solution.py:81
  142.2 2.5 %collective-permute-start = (bf16[2,256,384]{2,1,0:T(8,128)(2,1)}, bf16[2,256,384]{2,1,0:T(8,128)(2,1)}, u32[]{:S(2)}, u32[]{:S(2)}) collective-permute-start(bf16[2,256,384]{2,1,0:T(8,128)(2,1)} %fusion.28), channel_id=1, source_target_pairs={{0,16},{16,0},{1,17},{17,1},{2,18},{18,2},{3,19},{19,3},{4,20},{20... | collective-permute-start | bytes 1179656 | tf_op jit(solution)/shard_map/ppermute | solution.py:14
  142.9 21.5 %copy-start.14 = (f32[2,1536]{1,0:T(2,128)S(1)}, f32[2,1536]{1,0:T(2,128)}, u32[]{:S(2)}) copy-start(f32[2,1536]{1,0:T(2,128)} %get-tuple-element.32) | copy-start | bytes 36868
  143.0 21.7 %copy-start.11 = (bf16[1536,64]{0,1:T(8,128)(2,1)S(1)}, bf16[1536,64]{0,1:T(8,128)(2,1)}, u32[]{:S(2)}) copy-start(bf16[1536,64]{0,1:T(8,128)(2,1)} %param.22) | copy-start | bytes 589828
  144.7 20.6 %copy-start.16 = (f32[1,64,128]{2,1,0:T(8,128)S(1)}, f32[1,64,128]{2,1,0:T(8,128)}, u32[]{:S(2)}) copy-start(f32[1,64,128]{2,1,0:T(8,128)} %param.23) | copy-start | bytes 98308
Sparse Core Ops, SparseCore 0:
  102.1 36.2 reduce-scatter.3
where the time goes:
time: 176 us; the launch traced here: 175 us
  local copies, waits for them, and re-layouts  63.3 us (36%)
  waiting for transfers between devices  28.7 us (16%)
  matrix products  27.7 us (16%)
  blocking collectives  18 us (10%)
  between operations  14.4 us (8%)
  other arithmetic  13.4 us (8%)
  starting transfers between devices  9.07 us (5%)
    unnamed x2, waiting for transfers between devices  27.1 us
    unnamed x49, local copies, waits for them, and re-layouts  25.6 us
    all_gather x1, blocking collectives, shards(): final_rows = lax.all_gather(last_half, 'head', axis=2, tiled=True)  18 us
    dot_general x3, matrix products, piece_scores(): jnp.einsum('sqhd,skhd->shqk', query_heads, key_heads, preferred_element_t...  10.8 us
    dot_general x3, matrix products, piece_values(): jnp.einsum('shqk,skhd->sqhd', probs_piece, value_heads, preferred_element...  9.17 us
    another operation x1, local copies, waits for them, and re-layouts, piece_values(): value_heads = value_piece.reshape(seq_dev, -1, head_count, HEAD_DIM)  6.13 us
    another operation x1, local copies, waits for them, and re-layouts, piece_scores(): key_heads = key_piece.reshape(seq_dev, -1, head_count, HEAD_DIM)  6.03 us
    all_to_all x1, starting transfers between devices, shards(): lax.all_to_all(local_cache, 'blk', split_axis=0, concat_axis=1, tiled=True)  5.44 us
  transfers between devices with their start and end apart: 4, of which 2 were waited for; matrix products, arithmetic and copies ran while one was open for 27% of the time, Pallas kernels for 0%

commit v1 on v0

--- a/solution.py
+++ b/solution.py
@@ -7,6 +7,18 @@
 norm_eps = 1e-06
 guidance = 4.0
 euler_step = -0.25
+
+
+def split_up(shard, dim, size):
+    shape = shard.shape
+    blocks = shard.reshape(*shape[:dim], size, shape[dim] // size, *shape[dim + 1 :])
+    return jnp.moveaxis(blocks, dim, 0)
+
+
+def laid_out(blocks, dim):
+    dims = list(blocks.shape[1:])
+    dims[dim] *= blocks.shape[0]
+    return jnp.moveaxis(blocks, 0, dim).reshape(dims)
 
 
 def passed_along(shard, axis, by):
@@ -81,7 +93,14 @@
     refreshed = lax.all_to_all(fresh_kv, "blk", split_axis=1, concat_axis=0, tiled=True)
     local_cache = kv_cache[0]
     patch_count = local_cache.shape[2]
-    fetched = lax.all_to_all(local_cache, "blk", split_axis=0, concat_axis=1, tiled=True)
+    length, index = (lax.axis_size("blk"), lax.axis_index("blk"))
+    blocks = split_up(local_cache, 0, length)
+    outs = [blocks[index]]
+    for turn in range(1, length):
+        sent = blocks[index ^ turn]
+        outs.append(lax.ppermute(sent, "blk", [(i_2, i_2 ^ turn) for i_2 in range(length)]))
+    blocks = jnp.stack(outs)[index ^ jnp.arange(length)]
+    fetched = laid_out(blocks, 1)
     keep_patch = jnp.arange(patch_count, dtype=jnp.int32)[None, :] != own_patch[:, None]
     stale_counted = jnp.tile(keep_patch, (1, patch_rows))
     stale_keys = fetched[:, :, :, 0].reshape(seq_dev, -1, group_width)

time: 176 us -> 194 us (1.10)
  local copies, waits for them, and re-layouts: 63.3 us -> 76.3 us
  other arithmetic: 13.4 us -> 19.7 us
    gather x0 -> x1, local copies, waits for them, and re-layouts: none -> 10.5 us  [shards(): blocks = jnp.stack(outs)[index ^ jnp.arange(length)]]
    another operation x1 -> x2, other arithmetic: 0.69 us -> 8.91 us  [the longest x1 8.22 us: shards(): blocks = jnp.stack(outs)[index ^ jnp.arange(length)]]
    all_to_all x1 -> x0, starting transfers between devices: 5.44 us -> none  [shards(): lax.all_to_all(local_cache, 'blk', split_axis=0, concat_axis=1, tiled=True)]
    dynamic_slice x0 -> x1, local copies, waits for them, and re-layouts: none -> 4.71 us  [shards(): outs = [blocks[index]]]
    ppermute x0 -> x3, starting transfers between devices: none -> 4.47 us  [shards(): lax.ppermute(sent, 'blk', [(i_2, i_2 ^ turn) for i_2 in range(length)])]
    all_to_all x1 -> x0, local copies, waits for them, and re-layouts: 3.4 us -> none  [shards(): lax.all_to_all(local_cache, 'blk', split_axis=0, concat_axis=1, tiled=True)]
    transpose x0 -> x1, local copies, waits for them, and re-layouts: none -> 3.4 us  [laid_out(): return jnp.moveaxis(blocks, 0, dim).reshape(dims)]
    unnamed x49, local copies, waits for them, and re-layouts: 25.6 us -> 23.4 us
  transfers between devices with their start and end apart: 4 -> 6, of which waited for: 2 -> 1; matrix products, arithmetic and copies ran while one was open for 27% -> 24% of each run, Pallas kernels for 0% -> 0%
where the time goes in v1:
time: 194 us; the launch traced here: 192 us
  local copies, waits for them, and re-layouts  76.3 us (39%)
  matrix products  27.9 us (14%)
  waiting for transfers between devices  27.1 us (14%)
  other arithmetic  19.7 us (10%)
  blocking collectives  18 us (9%)
  between operations  14.5 us (7%)
  starting transfers between devices  8.9 us (5%)
    unnamed x2, waiting for transfers between devices  27.1 us
    unnamed x49, local copies, waits for them, and re-layouts  23.4 us
    all_gather x1, blocking collectives, shards(): final_rows = lax.all_gather(last_half, 'head', axis=2, tiled=True)  18 us
    dot_general x3, matrix products, piece_scores(): jnp.einsum('sqhd,skhd->shqk', query_heads, key_heads, preferred_element_t...  11 us
    gather x1, local copies, waits for them, and re-layouts, shards(): blocks = jnp.stack(outs)[index ^ jnp.arange(length)]  10.5 us
    dot_general x3, matrix products, piece_values(): jnp.einsum('shqk,skhd->sqhd', probs_piece, value_heads, preferred_element...  9.16 us
    another operation x1, other arithmetic, shards(): blocks = jnp.stack(outs)[index ^ jnp.arange(length)]  8.22 us
    another operation x1, local copies, waits for them, and re-layouts, piece_values(): value_heads = value_piece.reshape(seq_dev, -1, head_count, HEAD_DIM)  6.16 us
  transfers between devices with their start and end apart: 6, of which 1 were waited for; matrix products, arithmetic and copies ran while one was open for 24% of the time, Pallas kernels for 0%

profile of v1, /device:TPU:0, one launch (start us, length us, event | category | flops | bytes accessed | tf_op | source)
XLA Modules:
  0.0 192.4 jit_solution(14317392326401064994)
XLA Ops:
  7.3 4.7 %constant_dynamic-slice_fusion = (bf16[1,2,64,4,2,384]{5,4,3,2,1,0:T(2,128)(2,1)}, bf16[2,64,4,2,384]{4,3,2,1,0:T(2,128)(2,1)}, bf16[2,64,4,2,384]{4,3,2,1,0:T(2,128)(2,1)}, bf16[2,64,4,2,384]{4,3,2,1,0:T(2,128)(2,1)}) fusion(bf16[4,2,64,4,2,384]{5,4,3,2,1,0:T(2,128)(2,1)} %bitcast.100, s32[]{:T(128)S(6)} %select_n.56, s32[]{:T(128)S(6)} %select_n.59, ...), kind=kLoop, calls=%fused_computation.65 | loop fusion | bytes 6291472 | tf_op jit(solution)/shard_map/dynamic_slice | solution.py:98
  12.0 2.9 %collective-permute-start = (bf16[2,64,4,2,384]{4,3,2,1,0:T(2,128)(2,1)}, bf16[2,64,4,2,384]{4,3,2,1,0:T(2,128)(2,1)}, u32[]{:S(2)}, u32[]{:S(2)}) collective-permute-start(bf16[2,64,4,2,384]{4,3,2,1,0:T(2,128)(2,1)} %get-tuple-element.17), channel_id=1, source_target_pairs={{0,1},{1,0},{2,3},{3,2},{4,5},{5,4},{6,7},{7,6},{8,9},{9,8},{10,11... | collective-permute-start | bytes 2359304 | tf_op jit(solution)/shard_map/ppermute | solution.py:101
  14.9 1.5 collective-permute-start.1
  17.6 0.5 multiply_reduce_fusion
  18.1 6.1 %copy.85 = bf16[1,1536,3,384]{1,3,2,0:T(8,128)(2,1)} copy(bf16[1,1536,3,384]{3,1,2,0:T(8,128)(2,1)} %param.15) | data formatting | bytes 7077888 | tf_op args[3]
  24.3 0.7 add_convert_fusion
  24.9 5.3 %convolution_convert_fusion = bf16[512,1152]{1,0:T(8,128)(2,1)} fusion(bf16[512,1536]{1,0:T(8,128)(2,1)S(1)} %bitcast.105, bf16[1536,1152]{0,1:T(8,128)(2,1)} %bitcast.99), kind=kOutput, calls=%fused_computation.16 | convolution fusion | flops 1812529152 | bytes 6291456 | tf_op jit(solution)/shard_map/dot_general | solution.py:83
  30.2 2.4 %copy.86 = bf16[512,1152]{0,1:T(8,128)(2,1)} copy(bf16[512,1152]{1,0:T(8,128)(2,1)} %convolution_convert_fusion) | data formatting | bytes 2359296 | tf_op jit(solution)/shard_map/convert_element_type | solution.py:87
  32.6 3.7 %reshape.256 = bf16[2,256,3,384]{1,0,3,2:T(2,128)(2,1)} reshape(bf16[512,1152]{0,1:T(8,128)(2,1)} %copy.86) | data formatting | bytes 2359296 | tf_op jit(solution)/shard_map/reshape | solution.py:88
  36.3 2.1 %fusion.37 = (bf16[2,256,1,384]{1,0,3,2:T(2,128)(2,1)S(1)}, bf16[2,256,1,384]{1,0,3,2:T(2,128)(2,1)S(1)}, bf16[2,256,1,384]{1,0,3,2:T(2,128)(2,1)S(1)}) fusion(bf16[2,256,3,384]{1,0,3,2:T(2,128)(2,1)} %reshape.256), kind=kLoop, calls=%fused_computation.82 | loop fusion | bytes 2359296 | tf_op jit(solution)/shard_map/slice | solution.py:91
  38.5 0.8 copy.89
  39.3 1.6 fusion.38
  40.9 2.0 %copy.88 = bf16[2,154,1,384]{1,3,0,2:T(8,128)(2,1)} copy(bf16[2,154,1,384]{3,2,1,0:T(2,128)(2,1)} %get-tuple-element.22) | data formatting | bytes 473088 | tf_op jit(solution)/shard_map/slice | solution.py:113
  42.9 0.8 copy.93
  43.7 2.0 %copy.92 = bf16[2,154,1,384]{1,3,0,2:T(8,128)(2,1)} copy(bf16[2,154,1,384]{3,2,1,0:T(2,128)(2,1)} %get-tuple-element.21) | data formatting | bytes 473088 | tf_op jit(solution)/shard_map/slice | solution.py:135
  45.8 3.5 %fusion.9 = (f32[2,6,256]{2,1,0:T(8,128)}, f32[2,6,256,154]{2,3,1,0:T(8,128)}) fusion(pred[2,154]{1,0:T(4,128)(4,1)S(1)} %iota_compare_fusion, bf16[2,256,6,64]{1,3,2,0:T(8,128)(2,1)S(1)} %bitcast.96, bf16[2,154,6,64]{1,3,2,0:T(8,128)(2,1)} %bitcast.106), kind=kOutput, calls=%fused_computation.28 | convolution fusion | flops 61971456 | bytes 2534708 | tf_op jit(solution)/shard_map/sqhd,skhd->shqk/dot_general | solution.py:40
  49.4 2.9 %multiply_reduce_fusion.1 = (f32[2,6,256]{2,1,0:T(8,128)}, f32[2,6,256,256]{2,3,1,0:T(8,128)}) fusion(bf16[2,256,6,64]{1,3,2,0:T(8,128)(2,1)S(1)} %bitcast.97, bf16[2,256,6,64]{1,3,2,0:T(8,128)(2,1)S(1)} %bitcast.108), kind=kOutput, calls=%fused_computation.18 | convolution fusion | flops 102233088 | bytes 3944448 | tf_op jit(solution)/shard_map/sqhd,skhd->shqk/dot_general | solution.py:40
  52.3 8.2 %pad_maximum_fusion = bf16[4,2,64,4,2,384]{5,4,3,2,1,0:T(2,128)(2,1)} fusion(bf16[1,2,64,4,2,384]{5,4,3,2,1,0:T(2,128)(2,1)} %bitcast.17, bf16[1,2,64,4,2,384]{5,4,3,2,1,0:T(2,128)(2,1)} %bitcast.15, bf16[1,2,64,4,2,384]{5,4,3,2,1,0:T(2,128)(2,1)} %bitcast.13, bf16[1,2,64,4,2,384]{5,4,3,2,1,0:T(2,128)(2,1)S(1)} %copy-done.7), kind=kLoop, calls=%fused_computation.7 | loop fusion | flops 4718592 | bytes 6291456 | tf_op jit(solution)/shard_map/stack | solution.py:102
  60.5 10.5 %gather_fusion = bf16[4,2,64,4,2,384]{5,4,3,2,1,0:T(2,128)(2,1)} fusion(bf16[4,2,64,4,2,384]{5,4,3,2,1,0:T(2,128)(2,1)} %pad_maximum_fusion, s32[1024]{0:T(1024)S(1)} %pad_clamp_fusion), kind=kCustom, calls=%fused_computation | custom fusion | bytes 6291472 | tf_op jit(solution)/shard_map/gather | solution.py:102
  71.0 3.4 %copy.90 = bf16[2,4,64,4,2,384]{5,3,2,1,0,4:T(4,128)(2,1)S(1)} copy(bf16[2,4,64,4,2,384]{5,4,3,2,0,1:T(2,128)(2,1)} %bitcast.93) | data formatting | bytes 6291456 | tf_op jit(solution)/shard_map/transpose | solution.py:21
  74.4 2.7 %fusion.36 = (bf16[2,256,4,1,384]{4,2,1,0,3:T(4,128)(2,1)}, bf16[2,256,4,1,384]{4,2,1,0,3:T(4,128)(2,1)}) fusion(bf16[2,256,4,2,384]{4,2,1,0,3:T(4,128)(2,1)S(1)} %bitcast.92), kind=kLoop, calls=%fused_computation.81 | loop fusion | bytes 6291456 | tf_op jit(solution)/shard_map/slice | solution.py:107
  77.1 6.0 %reshape_reshape_squeeze.6 = bf16[2,1024,6,64]{3,2,1,0:T(8,128)(2,1)} reshape(bf16[2,256,4,1,384]{4,2,1,0,3:T(4,128)(2,1)} %get-tuple-element.13) | data formatting | bytes 3145728 | tf_op jit(solution)/shard_map/reshape;reshape;squeeze | solution.py:39
  83.1 4.6 %fusion = (f32[2,6,256]{2,1,0:T(8,128)S(1)}, f32[2,6,256,1024]{3,2,1,0:T(8,128)S(1)}) fusion(pred[2,1024]{1,0:T(4,128)(4,1)S(1)} %tile.9, bf16[2,256,6,64]{1,3,2,0:T(8,128)(2,1)S(1)} %bitcast.98, bf16[2,1024,6,64]{3,2,1,0:T(8,128)(2,1)} %reshape_reshape_squeeze.6), kind=kOutput, calls=%fused_computation.4 | convolution fusion | flops 412087296 | bytes 14563328 | tf_op jit(solution)/shard_map/sqhd,skhd->shqk/dot_general | solution.py:40
  87.8 0.5 fusion.6
  88.3 2.4 %copy-done.5 = f32[2,6,256,154]{2,3,1,0:T(8,128)S(1)} copy-done((f32[2,6,256,154]{2,3,1,0:T(8,128)S(1)}, f32[2,6,256,154]{2,3,1,0:T(8,128)}, u32[]{:S(2)}) %copy-start.5) | copy-done | bytes 1892376
  90.7 0.5 fusion.15
  91.2 3.1 %fusion.1 = f32[2,6,256]{2,1,0:T(8,128)S(1)} fusion(f32[2,6,256,1024]{3,2,1,0:T(8,128)S(1)} %get-tuple-element.28, f32[2,6,256]{2,1,0:T(8,128)S(1)} %maximum_maximum_fusion, pred[2,1024]{1,0:T(4,128)(4,1)S(1)} %tile.9), kind=kLoop, calls=%fused_computation.5 | loop fusion | flops 12579840 | bytes 12609536 | tf_op jit(solution)/shard_map/reduce_sum | solution.py:129
  94.3 6.2 %reshape_reshape_squeeze.7 = bf16[2,1024,6,64]{3,2,1,0:T(8,128)(2,1)} reshape(bf16[2,256,4,1,384]{4,2,1,0,3:T(4,128)(2,1)} %get-tuple-element.12) | data formatting | bytes 3145728 | tf_op jit(solution)/shard_map/reshape;reshape;squeeze | solution.py:50
  100.5 2.8 %fusion.16 = f32[2,256,6,64]{1,3,2,0:T(8,128)S(1)} fusion(bf16[2,256,6,64]{1,3,2,0:T(8,128)(2,1)S(1)} %bitcast.112, f32[2,6,256,256]{2,3,1,0:T(8,128)} %get-tuple-element.32, f32[2,6,256]{2,1,0:T(8,128)S(1)} %add_add_fusion, f32[2,6,256]{2,1,0:T(8,128)S(1)} %maximum_maximum_fusion), kind=kOutput, calls=%fused_computation.35 | convolution fusion | flops 103809024 | bytes 4349952 | tf_op jit(solution)/shard_map/shqk,skhd->sqhd/dot_general | solution.py:51
  103.3 2.7 %copy-done.2 = f32[2,6,256,1024]{3,2,1,0:T(8,128)S(1)} copy-done((f32[2,6,256,1024]{3,2,1,0:T(8,128)S(1)}, f32[2,6,256,1024]{3,2,1,0:T(8,128)}, u32[]{:S(2)}) %copy-start.2) | copy-done | bytes 12582936
  106.0 5.7 %fusion.19 = f32[2,256,6,64]{1,3,2,0:T(8,128)S(1)} fusion(f32[2,6,256,1024]{3,2,1,0:T(8,128)S(1)} %copy-done.2, f32[2,6,256]{2,1,0:T(8,128)S(1)} %add_add_fusion, f32[2,6,256]{2,1,0:T(8,128)S(1)} %maximum_maximum_fusion, pred[2,1024]{1,0:T(4,128)(4,1)S(1)} %tile.9, bf16[2,1024,6,64]{3,2,1,0:T(8,128)(2,1)} %reshape_reshape_squeeze.7), kind=kOutput, calls=%fused_computation.39 | convolution fusion | flops 418381824 | bytes 14968832 | tf_op jit(solution)/shard_map/shqk,skhd->sqhd/dot_general | solution.py:51
  111.7 0.7 fusion.22
  112.4 2.2 %convolution_convert_fusion.1 = bf16[2,256,1536]{2,1,0:T(8,128)(2,1)} fusion(bf16[2,256,384]{1,2,0:T(8,128)(2,1)S(1)} %bitcast.110, bf16[1,384,1536]{2,1,0:T(8,128)(2,1)S(1)} %copy-done), kind=kOutput, calls=%fused_computation.17 | convolution fusion | flops 604766208 | bytes 3145728 | tf_op jit(solution)/shard_map/dot_general | solution.py:140
  114.6 4.9 %copy.105 = bf16[2,256,1536]{1,0,2:T(2,128)(2,1)} copy(bf16[2,256,1536]{2,1,0:T(8,128)(2,1)} %convolution_convert_fusion.1) | data formatting | bytes 3145728
  119.5 3.0 %copy.111 = bf16[192,8,2,256]{3,1,2,0:T(8,128)(2,1)} copy(bf16[192,8,2,256]{3,2,1,0:T(2,128)(2,1)} %bitcast.95) | data formatting | bytes 3145728
  122.5 2.9 %copy.97 = bf16[2,256,2,384]{3,2,0,1:T(2,128)(2,1)} copy(bf16[2,256,2,384]{1,0,3,2:T(2,128)(2,1)S(1)} %slice-done) | data formatting | bytes 1572864 | tf_op jit(solution)/shard_map/stack | solution.py:92
  125.4 4.3 %all-to-all-start = ((bf16[2,256,2,384]{3,2,0,1:T(2,128)(2,1)}), bf16[2,256,2,384]{3,2,0,1:T(2,128)(2,1)S(1)}, u32[]{:S(2)}, u32[]{:S(2)}) async-start(bf16[2,256,2,384]{3,2,0,1:T(2,128)(2,1)} %copy.97), calls=%async_computation | async-start | bytes 1572864 | tf_op jit(solution)/shard_map/all_to_all | solution.py:93
  129.7 2.1 %convert_element_type.70 = f32[1,2,256,1536]{3,2,1,0:T(8,128)} convert(bf16[1,2,256,1536]{3,2,1,0:T(8,128)(2,1)S(1)} %copy-done.3) | non-fusion elementwise | flops 786432 | bytes 4718592 | tf_op jit(solution)/shard_map/convert_element_type | solution.py:77
  131.8 0.7 convert_bitcast_fusion
  132.5 27.1 %reduce-scatter.4.cloned.1.call-done = bf16[384,512]{1,0:T(8,128)(2,1)} async-done(((bf16[1536,512]{1,0:T(8,128)(2,1)}), bf16[384,512]{1,0:T(8,128)(2,1)}) %reduce-scatter.4.cloned.1.call-update) | async-done | bytes 393232
  159.6 1.1 reshape.272
  160.7 0.7 copy.106
  161.4 1.2 fusion.28
  163.0 1.7 copy.101
  164.7 18.0 %all_gather.3 = bf16[2,128,1536]{2,1,0:T(8,128)(2,1)S(1)} all-gather(bf16[2,128,384]{2,1,0:T(8,128)(2,1)S(1)} %dynamic-slice_select_fusion), channel_id=1, replica_groups=mesh['section'=2,'head'=4,'blk'=4] {'head'}, dimensions={2}, use_global_device_ids=true | all-gather | bytes 983040 | tf_op jit(solution)/shard_map/all_gather | solution.py:161
  183.3 0.4 fusion.13
  184.2 0.6 multiply_add_fusion
  184.9 0.7 copy.125
  (82 shorter events, 2.8 us)
Async XLA Ops:
  7.2 105.3 %copy-start = (bf16[1,384,1536]{2,1,0:T(8,128)(2,1)S(1)}, bf16[1,384,1536]{2,1,0:T(8,128)(2,1)}, u32[]{:S(2)}) copy-start(bf16[1,384,1536]{2,1,0:T(8,128)(2,1)} %param.16) | copy-start | bytes 3538948
  7.2 152.5 %reduce-scatter.4.cloned.1.call-start = ((), (), s32[]{:S(2)}) async-start(), calls=%async_computation.2 | async-start | bytes 1966080
  7.2 9.2 %copy-start.18 = (s32[4,4]{1,0:T(4,128)S(1)}, s32[4,4]{1,0:T(4,128)}, u32[]{:S(2)}) copy-start(s32[4,4]{1,0:T(4,128)} %param.20) | copy-start | bytes 196
  7.3 10.0 %copy-start.17 = (bf16[1,2,2,1536]{3,2,1,0:T(2,128)(2,1)S(1)}, bf16[1,2,2,1536]{3,2,1,0:T(2,128)(2,1)}, u32[]{:S(2)}) copy-start(bf16[1,2,2,1536]{3,2,1,0:T(2,128)(2,1)} %param.13) | copy-start | bytes 36868
  7.3 10.0 %copy-start.3 = (bf16[1,2,256,1536]{3,2,1,0:T(8,128)(2,1)S(1)}, bf16[1,2,256,1536]{3,2,1,0:T(8,128)(2,1)}, u32[]{:S(2)}) copy-start(bf16[1,2,256,1536]{3,2,1,0:T(8,128)(2,1)} %param.12) | copy-start | bytes 4718596
  12.0 40.2 %collective-permute-start = (bf16[2,64,4,2,384]{4,3,2,1,0:T(2,128)(2,1)}, bf16[2,64,4,2,384]{4,3,2,1,0:T(2,128)(2,1)}, u32[]{:S(2)}, u32[]{:S(2)}) collective-permute-start(bf16[2,64,4,2,384]{4,3,2,1,0:T(2,128)(2,1)} %get-tuple-element.17), channel_id=1, source_target_pairs={{0,1},{1,0},{2,3},{3,2},{4,5},{5,4},{6,7},{7,6},{8,9},{9,8},{10,11... | collective-permute-start | bytes 2359304 | tf_op jit(solution)/shard_map/ppermute | solution.py:101
  14.9 37.3 %collective-permute-start.1 = (bf16[2,64,4,2,384]{4,3,2,1,0:T(2,128)(2,1)}, bf16[2,64,4,2,384]{4,3,2,1,0:T(2,128)(2,1)}, u32[]{:S(2)}, u32[]{:S(2)}) collective-permute-start(bf16[2,64,4,2,384]{4,3,2,1,0:T(2,128)(2,1)} %get-tuple-element.16), channel_id=1, source_target_pairs={{0,2},{1,3},{2,0},{3,1},{4,6},{5,7},{6,4},{7,5},{8,10},{9,11},{10,... | collective-permute-start | bytes 2359304 | tf_op jit(solution)/shard_map/ppermute | solution.py:101
  16.4 35.8 %collective-permute-start.2 = (bf16[2,64,4,2,384]{4,3,2,1,0:T(2,128)(2,1)}, bf16[2,64,4,2,384]{4,3,2,1,0:T(2,128)(2,1)}, u32[]{:S(2)}, u32[]{:S(2)}) collective-permute-start(bf16[2,64,4,2,384]{4,3,2,1,0:T(2,128)(2,1)} %get-tuple-element.15), channel_id=1, source_target_pairs={{0,3},{1,2},{2,1},{3,0},{4,7},{5,6},{6,5},{7,4},{8,11},{9,10},{10,... | collective-permute-start | bytes 2359304 | tf_op jit(solution)/shard_map/ppermute | solution.py:101
  36.3 3.0 %copy-start.8 = (bf16[1,2,154,2,384]{4,3,2,1,0:T(2,128)(2,1)S(1)}, bf16[1,2,154,2,384]{4,3,2,1,0:T(2,128)(2,1)}, u32[]{:S(2)}) copy-start(bf16[1,2,154,2,384]{4,3,2,1,0:T(2,128)(2,1)} %param.18) | copy-start | bytes 1419268
  38.4 7.3 %copy-start.19 = (s32[2]{0:T(128)S(1)}, s32[2]{0:T(128)}, u32[]{:S(2)}) copy-start(s32[2]{0:T(128)} %param.19) | copy-start | bytes 28
  43.7 5.7 %copy-start.9 = (bf16[2,256,1,384]{1,3,0,2:T(8,128)(2,1)S(1)}, bf16[2,256,1,384]{1,3,0,2:T(8,128)(2,1)}, u32[]{:S(2)}) copy-start(bf16[2,256,1,384]{1,3,0,2:T(8,128)(2,1)} %copy.89) | copy-start | bytes 1179652
  45.8 6.4 %copy-start.7 = (bf16[1,2,64,4,2,384]{5,4,3,2,1,0:T(2,128)(2,1)S(1)}, bf16[1,2,64,4,2,384]{5,4,3,2,1,0:T(2,128)(2,1)}, u32[]{:S(2)}) copy-start(bf16[1,2,64,4,2,384]{5,4,3,2,1,0:T(2,128)(2,1)} %get-tuple-element.14) | copy-start | bytes 2359300
  83.1 4.6 %copy-start.13 = (f32[2,6,256]{2,1,0:T(8,128)S(1)}, f32[2,6,256]{2,1,0:T(8,128)}, u32[]{:S(2)}) copy-start(f32[2,6,256]{2,1,0:T(8,128)} %get-tuple-element.29) | copy-start | bytes 36868
  83.1 4.6 %copy-start.14 = (f32[2,6,256]{2,1,0:T(8,128)S(1)}, f32[2,6,256]{2,1,0:T(8,128)}, u32[]{:S(2)}) copy-start(f32[2,6,256]{2,1,0:T(8,128)} %get-tuple-element.31) | copy-start | bytes 36868
  83.1 4.6 %copy-start.4 = (f32[2,6,256,256]{2,3,1,0:T(8,128)S(1)}, f32[2,6,256,256]{2,3,1,0:T(8,128)}, u32[]{:S(2)}) copy-start(f32[2,6,256,256]{2,3,1,0:T(8,128)} %get-tuple-element.32) | copy-start | bytes 9437188
  87.7 6.6 %copy-start.1 = (f32[2,6,256,1024]{3,2,1,0:T(8,128)}, f32[2,6,256,1024]{3,2,1,0:T(8,128)S(1)}, u32[]{:S(2)}) copy-start(f32[2,6,256,1024]{3,2,1,0:T(8,128)S(1)} %get-tuple-element.28) | copy-start | bytes 37748740
  87.7 3.0 %copy-start.5 = (f32[2,6,256,154]{2,3,1,0:T(8,128)S(1)}, f32[2,6,256,154]{2,3,1,0:T(8,128)}, u32[]{:S(2)}) copy-start(f32[2,6,256,154]{2,3,1,0:T(8,128)} %get-tuple-element.30) | copy-start | bytes 5677060
  94.3 6.2 %copy-start.11 = (bf16[2,256,1,384]{1,3,0,2:T(8,128)(2,1)S(1)}, bf16[2,256,1,384]{1,3,0,2:T(8,128)(2,1)}, u32[]{:S(2)}) copy-start(bf16[2,256,1,384]{1,3,0,2:T(8,128)(2,1)} %copy.93) | copy-start | bytes 1179652
  100.5 5.5 %copy-start.2 = (f32[2,6,256,1024]{3,2,1,0:T(8,128)S(1)}, f32[2,6,256,1024]{3,2,1,0:T(8,128)}, u32[]{:S(2)}) copy-start(f32[2,6,256,1024]{3,2,1,0:T(8,128)} %copy-done.1) | copy-start | bytes 37748740
  106.0 5.7 %copy-start.6 = (f32[2,6,256,154]{2,3,1,0:T(8,128)S(1)}, f32[2,6,256,154]{2,3,1,0:T(8,128)}, u32[]{:S(2)}) copy-start(f32[2,6,256,154]{2,3,1,0:T(8,128)} %get-tuple-element.30) | copy-start | bytes 5677060
  106.0 5.7 %copy-start.10 = (bf16[2,154,1,384]{1,3,0,2:T(8,128)(2,1)S(1)}, bf16[2,154,1,384]{1,3,0,2:T(8,128)(2,1)}, u32[]{:S(2)}) copy-start(bf16[2,154,1,384]{1,3,0,2:T(8,128)(2,1)} %copy.92) | copy-start | bytes 709636
  119.5 3.0 %slice-start = ((bf16[2,256,3,384]{1,0,3,2:T(2,128)(2,1)}), bf16[2,256,2,384]{1,0,3,2:T(2,128)(2,1)S(1)}, s32[]{:S(2)}) async-start(bf16[2,256,3,384]{1,0,3,2:T(2,128)(2,1)} %reshape.256), calls=%async_computation.3 | async-start | bytes 1572864 | tf_op jit(solution)/shard_map/stack | solution.py:92
  125.4 6.4 %copy-start.15 = (bf16[2,2,1536]{2,1,0:T(2,128)(2,1)S(1)}, bf16[2,2,1536]{2,1,0:T(2,128)(2,1)}, u32[]{:S(2)}) copy-start(bf16[2,2,1536]{2,1,0:T(2,128)(2,1)} %param.21) | copy-start | bytes 36868
  125.4 37.4 %all-to-all-start = ((bf16[2,256,2,384]{3,2,0,1:T(2,128)(2,1)}), bf16[2,256,2,384]{3,2,0,1:T(2,128)(2,1)S(1)}, u32[]{:S(2)}, u32[]{:S(2)}) async-start(bf16[2,256,2,384]{3,2,0,1:T(2,128)(2,1)} %copy.97), calls=%async_computation | async-start | bytes 1572864 | tf_op jit(solution)/shard_map/all_to_all | solution.py:93
  162.7 2.0 %collective-permute-start.3 = (bf16[2,256,384]{2,1,0:T(8,128)(2,1)S(1)}, bf16[2,256,384]{2,1,0:T(8,128)(2,1)S(1)}, u32[]{:S(2)}, u32[]{:S(2)}) collective-permute-start(bf16[2,256,384]{2,1,0:T(8,128)(2,1)S(1)} %fusion.28), channel_id=1, source_target_pairs={{0,16},{16,0},{1,17},{17,1},{2,18},{18,2},{3,19},{19,3},{4,20},{20... | collective-permute-start | bytes 1179656 | tf_op jit(solution)/shard_map/ppermute | solution.py:26
  163.0 20.7 %copy-start.12 = (bf16[1536,64]{0,1:T(8,128)(2,1)S(1)}, bf16[1536,64]{0,1:T(8,128)(2,1)}, u32[]{:S(2)}) copy-start(bf16[1536,64]{0,1:T(8,128)(2,1)} %param.22) | copy-start | bytes 589828
  164.7 19.5 %copy-start.16 = (f32[1,64,128]{2,1,0:T(8,128)S(1)}, f32[1,64,128]{2,1,0:T(8,128)}, u32[]{:S(2)}) copy-start(f32[1,64,128]{2,1,0:T(8,128)} %param.23) | copy-start | bytes 98308
Sparse Core Ops, SparseCore 0:
  122.6 36.9 reduce-scatter.3
